TPU v7x, 128 devices: a whole 4x4x4 slice. The times are simulated.
128 devices in a mesh: space: 128 (over z, y, x, core).
Axes of the slice: x: 4, y: 4, z: 4, core: 2. Of those that a mesh axis runs over, the one named last changes fastest.
Arguments:
- feats: bfloat16 [196608, 256], P('space'), may hold values from -24 to 24
- nbr_brick: int32 [27, 196608], P(None, 'space'), may hold values from 0 to 31, as said below
- nbr_row: int32 [27, 196608], P(None, 'space'), may hold values from 0 to 63
- nbr_valid: int32 [27, 196608], P(None, 'space'), may hold values 0 or 1
- dest: int32 [196608, 1], P('space'), may hold values from 0 to 127; in each aligned block of 1536 rows (0 to 1535, 1536 to 3071, ...) at most 16 rows name the same one
- conv_weight: bfloat16 [27, 256, 256], replicated, may hold values from -0.078125 to 0.078125
- cpe_linear: bfloat16 [256, 256], replicated, may hold values from -0.375 to 0.375
- cpe_gain: float32 [256], replicated, may hold values from 0.1 to 1.9
- cpe_shift: float32 [256], replicated, may hold values from -2.5 to 2.5
- norm1_gain: float32 [256], replicated, may hold values from 0.1 to 1.9
- norm1_shift: float32 [256], replicated, may hold values from -2.5 to 2.5
- qkv_weight: bfloat16 [256, 768], replicated, may hold values from -4 to 4
- proj_weight: bfloat16 [256, 256], replicated, may hold values from -0.375 to 0.375
- norm2_gain: float32 [256], replicated, may hold values from 0.1 to 1.9
- norm2_shift: float32 [256], replicated, may hold values from -2.5 to 2.5
- fc1_weight: bfloat16 [256, 1024], replicated, may hold values from -0.375 to 0.375
- fc2_weight: bfloat16 [1024, 256], replicated, may hold values from -0.1875 to 0.1875
Outputs:
- block_output: bfloat16 [196608, 256], P('space')
Inputs may be any that keep to these rules, and one draw needn't show every extreme that they name: `dest`: the rows of one device name one owner at most 16 times; some device names some owner exactly 16 times. `nbr_brick`: for a row in the device's brick b (0 to 23) the value is b + 4 + d with d from -4 to 4; values below 4 name the lower device's last bricks, values from 28 the upper device's first bricks.
All inputs are finite; a program needn't handle non-finite values. No bound on the sum of `nbr_valid` on one device may be relied on, other than what follows from the above.
Results may differ from a plain program's by a relative error of at most 0.013.
The roundings to bfloat16 on the way count: a program that leaves them out, or rounds other values in their place, can miss the bound.
Values may be sent and summed in bfloat16 or wider, within the bound.
A program may use at most 128 MiB of HBM per device.

v0:
```python
import functools

import jax
import jax.numpy as jnp
from jax import lax
from jax.experimental import pallas as pl
from jax.experimental.pallas import tpu as pltpu
from jax.sharding import PartitionSpec as P

HEADS = 16
HEAD = 16
C = 256
PATCH = 1024
BR = 64
HB = 4
KOFF = 27
ROWS = 1536
GROUP = 256
WINDOW = 768
LOG2E = 1.4426950408889634
SAFE_SCORE = 60.0
EMPTY = 1024.0
F32 = jnp.float32
BF16 = jnp.bfloat16


def layer_norm(values, gain, shift):
    average = jnp.mean(values, axis=-1, keepdims=True)
    centred = values - average
    spread = jnp.mean(centred * centred, axis=-1, keepdims=True)
    return centred * lax.rsqrt(spread + 1e-05) * gain + shift


def to_wire(rows):
    shaped = rows.reshape(128, 8, C)
    return jnp.concatenate([shaped[:, :, :128], shaped[:, :, 128:]], axis=1).astype(BF16)


def from_wire(block):
    wide = block.astype(F32)
    return jnp.concatenate([wide[:, :8], wide[:, 8:]], axis=2).reshape(PATCH, C)


def encode_kernel(
    ext, brick, row, valid, dest, weight, linear, gain, shift,
    enriched, out0, out1, position,
    ext_t, weight_t, relative, picked,
):
    for i in range(8):
        ext_t[:, GROUP * i : GROUP * (i + 1)] = ext[GROUP * i : GROUP * (i + 1), :].T

    def turn_weight(k, carry):
        weight_t[:, pl.ds(pl.multiple_of(k * C, C), C)] = weight[k].T
        return carry

    lax.fori_loop(0, KOFF, turn_weight, 0)
    base = lax.broadcasted_iota(jnp.int32, (KOFF, ROWS), 1) // GROUP * GROUP
    relative[...] = jnp.where(valid[...] > 0, brick[...] * BR + row[...] - base, -1)
    place = lax.broadcasted_iota(jnp.int32, (WINDOW, 1), 0)

    def conv_group(g, carry):
        columns = pl.ds(pl.multiple_of(g * GROUP, GROUP), GROUP)
        window = ext_t[:, pl.ds(pl.multiple_of(g * GROUP, GROUP), WINDOW)]
        for k in range(KOFF):
            chosen = jnp.where(relative[k : k + 1, columns] == place, 1.0, 0.0).astype(BF16)
            picked[C * k : C * (k + 1), :] = jnp.dot(
                window, chosen, preferred_element_type=F32
            ).astype(BF16)
        summed = jnp.dot(weight_t[...], picked[...], preferred_element_type=F32)
        convolved = summed.astype(BF16).T
        projected = jnp.dot(convolved, linear[...], preferred_element_type=F32)
        own = ext[pl.ds(pl.multiple_of((g + 1) * GROUP, GROUP), GROUP), :].astype(F32)
        enriched[columns, :] = (own + layer_norm(projected, gain[...], shift[...])).astype(BF16)
        return carry

    lax.fori_loop(0, ROWS // GROUP, conv_group, 0)

    owner = lax.broadcasted_iota(jnp.int32, (128, 1), 0)
    before = jnp.where(
        lax.broadcasted_iota(jnp.int32, (GROUP, GROUP), 0)
        < lax.broadcasted_iota(jnp.int32, (GROUP, GROUP), 1), 1.0, 0.0,
    ).astype(BF16)
    count = jnp.zeros((128, 1), F32)
    for b in range(ROWS // GROUP):
        part = slice(GROUP * b, GROUP * (b + 1))
        target = dest[0:1, part]
        named = jnp.where(target == owner, 1.0, 0.0)
        running = jnp.dot(named.astype(BF16), before, preferred_element_type=F32) + count
        slot = jnp.sum(running * named, axis=0, keepdims=True).astype(jnp.int32)
        count = count + jnp.sum(named, axis=1, keepdims=True)
        position[0:1, part] = jnp.where(slot < 8, 0, PATCH) + target * 8 + slot % 8

    counts = jnp.broadcast_to(count, (128, 128)).astype(BF16)
    expand = jnp.where(
        lax.broadcasted_iota(jnp.int32, (PATCH, 128), 0) // 8
        == lax.broadcasted_iota(jnp.int32, (PATCH, 128), 1), 1.0, 0.0,
    ).astype(BF16)
    filled = jnp.dot(expand, counts, preferred_element_type=F32)
    filled = jnp.concatenate([filled, filled], axis=1)
    slots = (lax.broadcasted_iota(jnp.int32, (PATCH, C), 0) % 8).astype(F32)
    where_to = position[...]
    for patch, out in enumerate((out0, out1)):
        index = lax.broadcasted_iota(jnp.int32, (PATCH, 1), 0) + patch * PATCH
        chosen = jnp.where(index == where_to, 1.0, 0.0).astype(BF16)
        moved = jnp.dot(chosen, enriched[...], preferred_element_type=F32)
        out[...] = to_wire(jnp.where(slots + 8.0 * patch < filled, moved, EMPTY))


def attend_kernel(
    arrived, gain, shift, qkv_weight, proj, attended,
    keys, query_t, value_t, mixed_t,
):
    rows = from_wire(arrived[...])
    occupied = rows[:, 0:1] < 0.5 * EMPTY
    rows = jnp.where(occupied, rows, 0.0)
    normed = layer_norm(rows, gain[...], shift[...]).astype(BF16)
    qkv = jnp.dot(normed, qkv_weight[...], preferred_element_type=F32).astype(BF16)
    queries = qkv[:, :C]
    keys[...] = qkv[:, C : 2 * C]
    values = jnp.where(occupied, qkv[:, 2 * C :], BF16(0))
    ones = jnp.broadcast_to(jnp.where(occupied, 1.0, 0.0), (PATCH, 128)).astype(BF16).T

    member = jnp.where(
        lax.broadcasted_iota(jnp.int32, (C, 128), 0) // HEAD
        == lax.broadcasted_iota(jnp.int32, (C, 128), 1), 1.0, 0.0,
    ).astype(BF16)

    def largest_square(table):
        wide = table.astype(F32)
        squares = jnp.dot((wide * wide).astype(BF16), member, preferred_element_type=F32)
        return jnp.max(squares, axis=0, keepdims=True)

    bound = jnp.max(largest_square(queries) * largest_square(qkv[:, C : 2 * C])) / HEAD
    safe = bound < SAFE_SCORE * SAFE_SCORE

    turned = (queries * BF16(HEAD ** (-0.5))).T
    values_t = values.T
    channel = lax.broadcasted_iota(jnp.int32, (128, 1), 0) // HEAD
    for h in range(HEADS):
        half, inside = h // 8, h % 8
        query_t[h] = jnp.where(channel == inside, turned[128 * half : 128 * (half + 1), :], BF16(0))
        value_t[h, :HEAD] = values_t[HEAD * h : HEAD * (h + 1), :]
        value_t[h, HEAD:] = ones[:HEAD, :]

    def finish(h, products, columns):
        below = products[HEAD : HEAD + 1, :]
        below = jnp.where(below > 0, below, 1.0)
        mixed_t[h, :, columns] = (products[:HEAD, :] / below).astype(BF16)

    block = 512

    @pl.when(safe)
    def _():
        def step(t, carry):
            half, column = t // (PATCH // block), t % (PATCH // block)
            columns = pl.ds(pl.multiple_of(column * block, block), block)
            some = keys[:, pl.ds(pl.multiple_of(half * 128, 128), 128)]
            for inside in range(8):
                h = half * 8 + inside
                scores = jnp.dot(some, query_t[h, :, columns], preferred_element_type=F32)
                weights = jnp.exp2(scores * LOG2E).astype(BF16)
                finish(h, jnp.dot(value_t[h], weights, preferred_element_type=F32), columns)
            return carry

        lax.fori_loop(0, 2 * (PATCH // block), step, 0)

    @pl.when(jnp.logical_not(safe))
    def _():
        penalty = jnp.where(occupied, 0.0, -1e30)

        def step(t, carry):
            h, column = t // (PATCH // 128), t % (PATCH // 128)
            columns = pl.ds(pl.multiple_of(column * 128, 128), 128)
            some = keys[:, pl.ds(pl.multiple_of(h // 8 * 128, 128), 128)]
            scores = jnp.dot(some, query_t[h, :, columns], preferred_element_type=F32)
            scores = jnp.where(penalty < 0.0, penalty, scores)
            highest = jnp.max(scores, axis=0, keepdims=True)
            weights = jnp.exp(scores - highest).astype(BF16)
            finish(h, jnp.dot(value_t[h], weights, preferred_element_type=F32), columns)
            return carry

        lax.fori_loop(0, HEADS * (PATCH // 128), step, 0)

    mixed = mixed_t[...].reshape(C, PATCH).T
    attended[...] = to_wire(jnp.dot(mixed, proj[...], preferred_element_type=F32))


def finish_kernel(
    returned0, returned1, enriched, position, gain, shift, fc1, fc2, output, returned_t
):
    for patch, block in enumerate((returned0, returned1)):
        returned_t[:, PATCH * patch : PATCH * (patch + 1)] = from_wire(block[...]).astype(BF16).T
    index = lax.broadcasted_iota(jnp.int32, (2 * PATCH, 1), 0)
    for b in range(ROWS // GROUP):
        part = slice(GROUP * b, GROUP * (b + 1))
        chosen = jnp.where(position[0:1, part] == index, 1.0, 0.0).astype(BF16)
        home = jnp.dot(returned_t[...], chosen, preferred_element_type=F32).T
        residual = enriched[part, :].astype(F32) + home
        normed = layer_norm(residual, gain[...], shift[...]).astype(BF16)
        inner = jnp.dot(normed, fc1[...], preferred_element_type=F32)
        hidden = (0.5 * inner * (1.0 + lax.erf(inner * (0.5 ** 0.5)))).astype(BF16)
        output[part, :] = (
            residual + jnp.dot(hidden, fc2[...], preferred_element_type=F32)
        ).astype(BF16)


PARAMS = pltpu.CompilerParams(vmem_limit_bytes=56 * 2**20)
WIRE = jax.ShapeDtypeStruct((128, 16, 128), BF16)


def encode(ext, brick, row, valid, dest, weight, linear, gain, shift):
    return pl.pallas_call(
        encode_kernel,
        out_shape=(
            jax.ShapeDtypeStruct((ROWS, C), BF16), WIRE, WIRE,
            jax.ShapeDtypeStruct((1, ROWS), jnp.int32),
        ),
        scratch_shapes=[
            pltpu.VMEM((C, 2048), BF16),
            pltpu.VMEM((C, KOFF * C), BF16),
            pltpu.VMEM((KOFF, ROWS), jnp.int32),
            pltpu.VMEM((KOFF * C, GROUP), BF16),
        ],
        compiler_params=PARAMS,
        name="encode",
    )(ext, brick, row, valid, dest, weight, linear, gain, shift)


def attend(arrived, gain, shift, qkv_weight, proj):
    return pl.pallas_call(
        attend_kernel,
        out_shape=WIRE,
        scratch_shapes=[
            pltpu.VMEM((PATCH, C), BF16),
            pltpu.VMEM((HEADS, 128, PATCH), BF16),
            pltpu.VMEM((HEADS, 2 * HEAD, PATCH), BF16),
            pltpu.VMEM((HEADS, HEAD, PATCH), BF16),
        ],
        compiler_params=PARAMS,
        cost_estimate=pl.CostEstimate(flops=20 * 10**9, bytes_accessed=2**21, transcendentals=2**24),
        name="attend",
    )(arrived, gain, shift, qkv_weight, proj)


def finish(returned0, returned1, enriched, position, gain, shift, fc1, fc2):
    return pl.pallas_call(
        finish_kernel,
        out_shape=jax.ShapeDtypeStruct((ROWS, C), BF16),
        scratch_shapes=[pltpu.VMEM((C, 2 * PATCH), BF16)],
        compiler_params=PARAMS,
        name="finish",
    )(returned0, returned1, enriched, position, gain, shift, fc1, fc2)


def exchange(block):
    return lax.all_to_all(block, "space", split_axis=0, concat_axis=0, tiled=True)


def padded(block, width):
    count = lax.axis_size("space")
    forward = [(i, i + 1) for i in range(count - 1)]
    backward = [(i + 1, i) for i in range(count - 1)]
    low = lax.ppermute(block[block.shape[0] - width :], "space", forward)
    high = lax.ppermute(block[:width], "space", backward)
    return jnp.concatenate([low, block, high], axis=0)


def per_device(
    feats, nbr_brick, nbr_row, nbr_valid, dest, conv_weight, cpe_linear, cpe_gain, cpe_shift,
    norm1_gain, norm1_shift, qkv_weight, proj_weight, norm2_gain, norm2_shift, fc1_weight,
    fc2_weight,
):
    line = lambda v: v.reshape(1, C)
    ext = padded(feats, HB * BR)
    enriched, out0, out1, position = encode(
        ext, nbr_brick, nbr_row, nbr_valid, dest.reshape(1, ROWS), conv_weight, cpe_linear,
        line(cpe_gain), line(cpe_shift),
    )
    back = []
    arrived = [exchange(out0), exchange(out1)]
    for block in arrived:
        back.append(exchange(
            attend(block, line(norm1_gain), line(norm1_shift), qkv_weight, proj_weight)
        ))
    return finish(
        back[0], back[1], enriched, position, line(norm2_gain), line(norm2_shift), fc1_weight,
        fc2_weight,
    )


def solution(mesh):
    placed = (
        P("space", None), P(None, "space"), P(None, "space"), P(None, "space"), P("space", None),
        P(), P(), P(), P(), P(), P(), P(), P(), P(), P(), P(), P(),
    )
    return jax.shard_map(
        per_device, mesh=mesh, in_specs=placed, out_specs=P("space", None), check_vma=False
    )
```

profile of v0, /device:TPU:1, one launch (start us, length us, event | category | flops | bytes accessed | tf_op | source)
XLA Modules:
  0.0 278.4 jit_solution(5635193068597707270)
XLA Ops:
  0.0 1.0 fusion
  1.0 4.5 %collective-permute-start = (bf16[256,256]{1,0:T(8,128)(2,1)S(1)}, bf16[256,256]{1,0:T(8,128)(2,1)S(1)}, u32[]{:S(2)}, u32[]{:S(2)}) collective-permute-start(bf16[256,256]{1,0:T(8,128)(2,1)S(1)} %get-tuple-element.13), channel_id=1, source_target_pairs={{0,1},{1,2},{2,3},{3,4},{4,5},{5,6},{6,7},{7,8},{8,9},{9,10},{10,1... | collective-permute-start | bytes 393224 | tf_op jit(solution)/shard_map/ppermute | solution.py:263
  5.5 1.9 collective-permute-start.1
  7.4 0.0 collective-permute-done
  7.4 4.3 %collective-permute-done.1 = bf16[256,256]{1,0:T(8,128)(2,1)S(1)} collective-permute-done((bf16[256,256]{1,0:T(8,128)(2,1)S(1)}, bf16[256,256]{1,0:T(8,128)(2,1)S(1)}, u32[]{:S(2)}, u32[]{:S(2)}) %collective-permute-start.1) | collective-permute-done | bytes 131104 | tf_op jit(solution)/shard_map/ppermute | solution.py:264
  11.8 2.2 pad_maximum_fusion.ext
  14.0 35.0 %encode.1 = (bf16[1536,256]{1,0:T(8,128)(2,1)}, bf16[128,16,128]{2,1,0:T(8,128)(2,1)}, bf16[128,16,128]{2,1,0:T(8,128)(2,1)}, s32[1,1536]{1,0:T(1,128)}) custom-call(bf16[2048,256]{1,0:T(8,128)(2,1)} %pad_maximum_fusion.ext, s32[27,1536]{1,0:T(8,128)} %brick.1, s32[27,1536]{1,0:T(8,128)} %row.1, s32[27,1536]{1,0:T(8,128)} %valid.1, s32[1,1536]{1,0:T(1,128)} %bitcast.7, ...), custom_call_target="tpu_custom_call" | custom-call | tf_op jit(solution)/shard_map/encode/pallas_call | solution.py:212
  48.9 27.3 %all_to_all.20.arrived = bf16[128,16,128]{2,1,0:T(8,128)(2,1)} all-to-all(bf16[128,16,128]{2,1,0:T(8,128)(2,1)} %get-tuple-element.9), channel_id=1, replica_groups=mesh['space'=128] {'space'}, dimensions={0} | all-to-all | bytes 1048576 | tf_op jit(solution)/shard_map/all_to_all | solution.py:256
  76.2 4.5 %all-to-all-start.2 = ((bf16[128,16,128]{2,1,0:T(8,128)(2,1)}), bf16[128,16,128]{2,1,0:T(8,128)(2,1)S(1)}, u32[]{:S(2)}, u32[]{:S(2)}) async-start(bf16[128,16,128]{2,1,0:T(8,128)(2,1)} %get-tuple-element.10), calls=%async_computation.2 | async-start | bytes 1048576 | tf_op jit(solution)/shard_map/all_to_all | solution.py:256
  80.7 78.6 %attend.2 = bf16[128,16,128]{2,1,0:T(8,128)(2,1)} custom-call(bf16[128,16,128]{2,1,0:T(8,128)(2,1)} %all_to_all.20.arrived, f32[1,256]{1,0:T(1,128)} %bitcast.12, f32[1,256]{1,0:T(1,128)} %bitcast.14, bf16[256,768]{1,0:T(8,128)(2,1)} %qkv_weight.3, bf16[256,256]{1,0:T(8,128)(2,1)} %proj.3), custom_call_target="tpu_custom_call" | custom-call | flops 20000000000 | bytes 2097152 | tf_op jit(solution)/shard_map/attend/pallas_call | solution.py:230
  159.3 0.0 all-to-all-done.2.arrived
  159.3 0.0 copy-start.1
  159.3 9.8 %all-to-all-start.1 = ((bf16[128,16,128]{2,1,0:T(8,128)(2,1)}), bf16[128,16,128]{2,1,0:T(8,128)(2,1)S(1)}, u32[]{:S(2)}, u32[]{:S(2)}) async-start(bf16[128,16,128]{2,1,0:T(8,128)(2,1)} %attend.2), calls=%async_computation.1 | async-start | bytes 1048576 | tf_op jit(solution)/shard_map/all_to_all | solution.py:256
  169.1 0.0 copy-done.1
  169.1 78.5 %attend.3 = bf16[128,16,128]{2,1,0:T(8,128)(2,1)} custom-call(bf16[128,16,128]{2,1,0:T(8,128)(2,1)} %copy-done.1, f32[1,256]{1,0:T(1,128)} %bitcast.13, f32[1,256]{1,0:T(1,128)} %bitcast.15, bf16[256,768]{1,0:T(8,128)(2,1)} %qkv_weight.3, bf16[256,256]{1,0:T(8,128)(2,1)} %proj.3), custom_call_target="tpu_custom_call" | custom-call | flops 20000000000 | bytes 2097152 | tf_op jit(solution)/shard_map/attend/pallas_call | solution.py:230
  247.6 0.0 all-to-all-done.1.returned0
  247.6 0.0 copy-start
  247.6 23.6 %all_to_all.21.returned1 = bf16[128,16,128]{2,1,0:T(8,128)(2,1)} all-to-all(bf16[128,16,128]{2,1,0:T(8,128)(2,1)} %attend.3), channel_id=1, replica_groups=mesh['space'=128] {'space'}, dimensions={0} | all-to-all | bytes 1048576 | tf_op jit(solution)/shard_map/all_to_all | solution.py:256
  271.2 0.0 copy-done
  271.2 7.2 %finish.1 = bf16[1536,256]{1,0:T(8,128)(2,1)} custom-call(bf16[128,16,128]{2,1,0:T(8,128)(2,1)} %copy-done, bf16[128,16,128]{2,1,0:T(8,128)(2,1)} %all_to_all.21.returned1, bf16[1536,256]{1,0:T(8,128)(2,1)} %get-tuple-element.11.enriched, s32[1,1536]{1,0:T(1,128)} %get-tuple-element.12.position, f32[1,256]{1,0:T(1,128)} %bitcast.8, f32[1,256]{1,0:T(1,128)} %bitcast.9, ...), custom_call_target="tpu_custom_call" | custom-call | tf_op jit(solution)/shard_map/finish/pallas_call | solution.py:246
Async XLA Ops:
  1.0 6.4 %collective-permute-start = (bf16[256,256]{1,0:T(8,128)(2,1)S(1)}, bf16[256,256]{1,0:T(8,128)(2,1)S(1)}, u32[]{:S(2)}, u32[]{:S(2)}) collective-permute-start(bf16[256,256]{1,0:T(8,128)(2,1)S(1)} %get-tuple-element.13), channel_id=1, source_target_pairs={{0,1},{1,2},{2,3},{3,4},{4,5},{5,6},{6,7},{7,8},{8,9},{9,10},{10,1... | collective-permute-start | bytes 393224 | tf_op jit(solution)/shard_map/ppermute | solution.py:263
  5.5 6.3 %collective-permute-start.1 = (bf16[256,256]{1,0:T(8,128)(2,1)S(1)}, bf16[256,256]{1,0:T(8,128)(2,1)S(1)}, u32[]{:S(2)}, u32[]{:S(2)}) collective-permute-start(bf16[256,256]{1,0:T(8,128)(2,1)S(1)} %get-tuple-element.14), channel_id=1, source_target_pairs={{1,0},{2,1},{3,2},{4,3},{5,4},{6,5},{7,6},{8,7},{9,8},{10,9},{11,1... | collective-permute-start | bytes 393224 | tf_op jit(solution)/shard_map/ppermute | solution.py:264
  76.2 83.1 %all-to-all-start.2 = ((bf16[128,16,128]{2,1,0:T(8,128)(2,1)}), bf16[128,16,128]{2,1,0:T(8,128)(2,1)S(1)}, u32[]{:S(2)}, u32[]{:S(2)}) async-start(bf16[128,16,128]{2,1,0:T(8,128)(2,1)} %get-tuple-element.10), calls=%async_computation.2 | async-start | bytes 1048576 | tf_op jit(solution)/shard_map/all_to_all | solution.py:256
  159.3 9.8 %copy-start.1 = (bf16[128,16,128]{2,1,0:T(8,128)(2,1)}, bf16[128,16,128]{2,1,0:T(8,128)(2,1)S(1)}, u32[]{:S(2)}) copy-start(bf16[128,16,128]{2,1,0:T(8,128)(2,1)S(1)} %all-to-all-done.2.arrived) | copy-start | bytes 1572868
  159.3 88.2 %all-to-all-start.1 = ((bf16[128,16,128]{2,1,0:T(8,128)(2,1)}), bf16[128,16,128]{2,1,0:T(8,128)(2,1)S(1)}, u32[]{:S(2)}, u32[]{:S(2)}) async-start(bf16[128,16,128]{2,1,0:T(8,128)(2,1)} %attend.2), calls=%async_computation.1 | async-start | bytes 1048576 | tf_op jit(solution)/shard_map/all_to_all | solution.py:256
  247.6 23.6 %copy-start = (bf16[128,16,128]{2,1,0:T(8,128)(2,1)}, bf16[128,16,128]{2,1,0:T(8,128)(2,1)S(1)}, u32[]{:S(2)}) copy-start(bf16[128,16,128]{2,1,0:T(8,128)(2,1)S(1)} %all-to-all-done.1.returned0) | copy-start | bytes 1572868
where the time goes:
time: 279 us; the launch traced here: 278 us
  Pallas kernels  199 us (71%)
  blocking collectives  50.9 us (18%)
  starting transfers between devices  20.7 us (7%)
  waiting for transfers between devices  4.36 us (2%)
    pallas_call x2, Pallas kernels, attend(): pl.pallas_call(attend_kernel, out_shape=WIRE, scratch_shapes=[pltpu.VMEM(...  157 us
    all_to_all x2, blocking collectives, exchange(): lax.all_to_all(block, 'space', split_axis=0, concat_axis=0, tiled=True)  50.9 us
    pallas_call x1, Pallas kernels, encode(): pl.pallas_call(encode_kernel, out_shape=(jax.ShapeDtypeStruct((ROWS, C),...  35 us
    all_to_all x2, starting transfers between devices, exchange(): lax.all_to_all(block, 'space', split_axis=0, concat_axis=0, tiled=True)  14.3 us
    pallas_call x1, Pallas kernels, finish(): pl.pallas_call(finish_kernel, out_shape=jax.ShapeDtypeStruct((ROWS, C), B...  7.18 us
  transfers between devices with their start and end apart: 4, of which 1 were waited for; matrix products, arithmetic and copies ran while one was open for 0% of the time, Pallas kernels for 56%

commit v1 on v0

--- a/solution.py
+++ b/solution.py
@@ -14,6 +14,7 @@
 BR = 64
 HB = 4
 KOFF = 27
+DEVICES = 128
 ROWS = 1536
 GROUP = 256
 WINDOW = 768
@@ -41,13 +42,52 @@
     return jnp.concatenate([wide[:, :8], wide[:, 8:]], axis=2).reshape(PATCH, C)
 
 
+def greet(barrier):
+    me = lax.axis_index("space")
+
+    def signal(step, carry):
+        pl.semaphore_signal(
+            barrier, inc=1, device_id=(lax.rem(me + step, DEVICES),),
+            device_id_type=pl.DeviceIdType.MESH,
+        )
+        return carry
+
+    lax.fori_loop(1, DEVICES, signal, 0)
+
+
+def send_all(source, target, send_sem, recv_sem):
+    me = lax.axis_index("space")
+
+    def start(step, carry):
+        other = lax.rem(me + step, DEVICES)
+        pltpu.make_async_remote_copy(
+            src_ref=source.at[other], dst_ref=target.at[me], send_sem=send_sem, recv_sem=recv_sem,
+            device_id=(other,), device_id_type=pl.DeviceIdType.MESH,
+        ).start()
+        return carry
+
+    lax.fori_loop(1, DEVICES, start, 0)
+    pltpu.make_async_copy(source.at[me], target.at[me], recv_sem).start()
+
+
+def wait_all(source, target, send_sem, recv_sem):
+    sent = source.at[pl.ds(0, DEVICES - 1)]
+    pltpu.make_async_copy(sent, sent, send_sem).wait()
+    pltpu.make_async_copy(target, target, recv_sem).wait()
+
+
 def encode_kernel(
-    ext, brick, row, valid, dest, weight, linear, gain, shift,
-    enriched, out0, out1, position,
-    ext_t, weight_t, relative, picked,
+    feats, brick, row, valid, dest, weight, linear, gain, shift,
+    enriched, arrived0, arrived1, position,
+    ext_t, weight_t, relative, picked, low, high, out0, out1, send_sem, recv_sem,
 ):
-    for i in range(8):
-        ext_t[:, GROUP * i : GROUP * (i + 1)] = ext[GROUP * i : GROUP * (i + 1), :].T
+    me = lax.axis_index("space")
+    barrier = pltpu.get_barrier_semaphore()
+    greet(barrier)
+
+    own_t = HB * BR // GROUP
+    for i in range(ROWS // GROUP):
+        ext_t[:, GROUP * (i + own_t) : GROUP * (i + own_t + 1)] = feats[GROUP * i : GROUP * (i + 1), :].T
 
     def turn_weight(k, carry):
         weight_t[:, pl.ds(pl.multiple_of(k * C, C), C)] = weight[k].T
@@ -55,10 +95,14 @@
 
     lax.fori_loop(0, KOFF, turn_weight, 0)
     base = lax.broadcasted_iota(jnp.int32, (KOFF, ROWS), 1) // GROUP * GROUP
-    relative[...] = jnp.where(valid[...] > 0, brick[...] * BR + row[...] - base, -1)
+    reach = brick[...] * BR + row[...]
+    lowest = jnp.where(me == 0, HB * BR, 0)
+    highest = jnp.where(me == DEVICES - 1, ROWS + HB * BR, ROWS + 2 * HB * BR)
+    counted = (valid[...] > 0) & (reach >= lowest) & (reach < highest)
+    relative[...] = jnp.where(counted, reach - base, -1)
     place = lax.broadcasted_iota(jnp.int32, (WINDOW, 1), 0)
 
-    def conv_group(g, carry):
+    def conv_group(g):
         columns = pl.ds(pl.multiple_of(g * GROUP, GROUP), GROUP)
         window = ext_t[:, pl.ds(pl.multiple_of(g * GROUP, GROUP), WINDOW)]
         for k in range(KOFF):
@@ -69,11 +113,39 @@
         summed = jnp.dot(weight_t[...], picked[...], preferred_element_type=F32)
         convolved = summed.astype(BF16).T
         projected = jnp.dot(convolved, linear[...], preferred_element_type=F32)
-        own = ext[pl.ds(pl.multiple_of((g + 1) * GROUP, GROUP), GROUP), :].astype(F32)
+        own = feats[columns, :].astype(F32)
         enriched[columns, :] = (own + layer_norm(projected, gain[...], shift[...])).astype(BF16)
-        return carry
-
-    lax.fori_loop(0, ROWS // GROUP, conv_group, 0)
+
+    def inner_group(g, carry):
+        conv_group(g)
+        return carry
+
+    lax.fori_loop(1, 3, inner_group, 0)
+    pl.semaphore_wait(barrier, DEVICES - 1)
+    width = HB * BR
+    up = pltpu.make_async_remote_copy(
+        src_ref=feats.at[pl.ds(ROWS - width, width)], dst_ref=low, send_sem=send_sem.at[2],
+        recv_sem=recv_sem.at[2], device_id=(lax.rem(me + 1, DEVICES),),
+        device_id_type=pl.DeviceIdType.MESH,
+    )
+    down = pltpu.make_async_remote_copy(
+        src_ref=feats.at[pl.ds(0, width)], dst_ref=high, send_sem=send_sem.at[3],
+        recv_sem=recv_sem.at[3], device_id=(lax.rem(me + DEVICES - 1, DEVICES),),
+        device_id_type=pl.DeviceIdType.MESH,
+    )
+    up.start()
+    down.start()
+    lax.fori_loop(3, 5, inner_group, 0)
+    up.wait()
+    down.wait()
+    ext_t[:, :GROUP] = low[...].T
+    ext_t[:, ROWS + GROUP :] = high[...].T
+
+    def outer_group(i, carry):
+        conv_group(i * (ROWS // GROUP - 1))
+        return carry
+
+    lax.fori_loop(0, 2, outer_group, 0)
 
     owner = lax.broadcasted_iota(jnp.int32, (128, 1), 0)
     before = jnp.where(
@@ -104,6 +176,10 @@
         chosen = jnp.where(index == where_to, 1.0, 0.0).astype(BF16)
         moved = jnp.dot(chosen, enriched[...], preferred_element_type=F32)
         out[...] = to_wire(jnp.where(slots + 8.0 * patch < filled, moved, EMPTY))
+        arrived = (arrived0, arrived1)[patch]
+        send_all(out, arrived, send_sem.at[patch], recv_sem.at[patch])
+    wait_all(out0, arrived0, send_sem.at[0], recv_sem.at[0])
+    wait_all(out1, arrived1, send_sem.at[1], recv_sem.at[1])
 
 
 def attend_kernel(
@@ -186,15 +262,25 @@
 
 
 def finish_kernel(
-    returned0, returned1, enriched, position, gain, shift, fc1, fc2, output, returned_t
+    attended0, attended1, enriched, position, gain, shift, fc1, fc2, output,
+    returned0, returned1, returned_t, chosen, send_sem, recv_sem,
 ):
-    for patch, block in enumerate((returned0, returned1)):
-        returned_t[:, PATCH * patch : PATCH * (patch + 1)] = from_wire(block[...]).astype(BF16).T
+    barrier = pltpu.get_barrier_semaphore()
+    greet(barrier)
+    pl.semaphore_wait(barrier, DEVICES - 1)
+    send_all(attended0, returned0, send_sem.at[0], recv_sem.at[0])
+    send_all(attended1, returned1, send_sem.at[1], recv_sem.at[1])
     index = lax.broadcasted_iota(jnp.int32, (2 * PATCH, 1), 0)
     for b in range(ROWS // GROUP):
         part = slice(GROUP * b, GROUP * (b + 1))
-        chosen = jnp.where(position[0:1, part] == index, 1.0, 0.0).astype(BF16)
-        home = jnp.dot(returned_t[...], chosen, preferred_element_type=F32).T
+        chosen[:, part] = jnp.where(position[0:1, part] == index, 1.0, 0.0).astype(BF16)
+    wait_all(attended0, returned0, send_sem.at[0], recv_sem.at[0])
+    wait_all(attended1, returned1, send_sem.at[1], recv_sem.at[1])
+    for patch, block in enumerate((returned0, returned1)):
+        returned_t[:, PATCH * patch : PATCH * (patch + 1)] = from_wire(block[...]).astype(BF16).T
+    for b in range(ROWS // GROUP):
+        part = slice(GROUP * b, GROUP * (b + 1))
+        home = jnp.dot(returned_t[...], chosen[:, part], preferred_element_type=F32).T
         residual = enriched[part, :].astype(F32) + home
         normed = layer_norm(residual, gain[...], shift[...]).astype(BF16)
         inner = jnp.dot(normed, fc1[...], preferred_element_type=F32)
@@ -204,11 +290,18 @@
         ).astype(BF16)
 
 
+def remote_params(number):
+    return pltpu.CompilerParams(
+        collective_id=number, has_side_effects=True, vmem_limit_bytes=56 * 2**20
+    )
+
+
+VMEM = pl.BlockSpec(memory_space=pltpu.VMEM)
 PARAMS = pltpu.CompilerParams(vmem_limit_bytes=56 * 2**20)
 WIRE = jax.ShapeDtypeStruct((128, 16, 128), BF16)
 
 
-def encode(ext, brick, row, valid, dest, weight, linear, gain, shift):
+def encode(feats, brick, row, valid, dest, weight, linear, gain, shift):
     return pl.pallas_call(
         encode_kernel,
         out_shape=(
@@ -220,10 +313,18 @@
             pltpu.VMEM((C, KOFF * C), BF16),
             pltpu.VMEM((KOFF, ROWS), jnp.int32),
             pltpu.VMEM((KOFF * C, GROUP), BF16),
+            pltpu.VMEM((HB * BR, C), BF16),
+            pltpu.VMEM((HB * BR, C), BF16),
+            pltpu.VMEM((128, 16, 128), BF16),
+            pltpu.VMEM((128, 16, 128), BF16),
+            pltpu.SemaphoreType.DMA((4,)),
+            pltpu.SemaphoreType.DMA((4,)),
         ],
-        compiler_params=PARAMS,
+        in_specs=[VMEM] * 9,
+        out_specs=[VMEM] * 4,
+        compiler_params=remote_params(0),
         name="encode",
-    )(ext, brick, row, valid, dest, weight, linear, gain, shift)
+    )(feats, brick, row, valid, dest, weight, linear, gain, shift)
 
 
 def attend(arrived, gain, shift, qkv_weight, proj):
@@ -242,27 +343,23 @@
     )(arrived, gain, shift, qkv_weight, proj)
 
 
-def finish(returned0, returned1, enriched, position, gain, shift, fc1, fc2):
+def finish(attended0, attended1, enriched, position, gain, shift, fc1, fc2):
     return pl.pallas_call(
         finish_kernel,
         out_shape=jax.ShapeDtypeStruct((ROWS, C), BF16),
-        scratch_shapes=[pltpu.VMEM((C, 2 * PATCH), BF16)],
-        compiler_params=PARAMS,
+        scratch_shapes=[
+            pltpu.VMEM((128, 16, 128), BF16),
+            pltpu.VMEM((128, 16, 128), BF16),
+            pltpu.VMEM((C, 2 * PATCH), BF16),
+            pltpu.VMEM((2 * PATCH, ROWS), BF16),
+            pltpu.SemaphoreType.DMA((2,)),
+            pltpu.SemaphoreType.DMA((2,)),
+        ],
+        in_specs=[VMEM] * 8,
+        out_specs=VMEM,
+        compiler_params=remote_params(1),
         name="finish",
-    )(returned0, returned1, enriched, position, gain, shift, fc1, fc2)
-
-
-def exchange(block):
-    return lax.all_to_all(block, "space", split_axis=0, concat_axis=0, tiled=True)
-
-
-def padded(block, width):
-    count = lax.axis_size("space")
-    forward = [(i, i + 1) for i in range(count - 1)]
-    backward = [(i + 1, i) for i in range(count - 1)]
-    low = lax.ppermute(block[block.shape[0] - width :], "space", forward)
-    high = lax.ppermute(block[:width], "space", backward)
-    return jnp.concatenate([low, block, high], axis=0)
+    )(attended0, attended1, enriched, position, gain, shift, fc1, fc2)
 
 
 def per_device(
@@ -271,19 +368,16 @@
     fc2_weight,
 ):
     line = lambda v: v.reshape(1, C)
-    ext = padded(feats, HB * BR)
-    enriched, out0, out1, position = encode(
-        ext, nbr_brick, nbr_row, nbr_valid, dest.reshape(1, ROWS), conv_weight, cpe_linear,
+    enriched, arrived0, arrived1, position = encode(
+        feats, nbr_brick, nbr_row, nbr_valid, dest.reshape(1, ROWS), conv_weight, cpe_linear,
         line(cpe_gain), line(cpe_shift),
     )
-    back = []
-    arrived = [exchange(out0), exchange(out1)]
-    for block in arrived:
-        back.append(exchange(
-            attend(block, line(norm1_gain), line(norm1_shift), qkv_weight, proj_weight)
-        ))
+    attended0, attended1 = [
+        attend(block, line(norm1_gain), line(norm1_shift), qkv_weight, proj_weight)
+        for block in (arrived0, arrived1)
+    ]
     return finish(
-        back[0], back[1], enriched, position, line(norm2_gain), line(norm2_shift), fc1_weight,
+        attended0, attended1, enriched, position, line(norm2_gain), line(norm2_shift), fc1_weight,
         fc2_weight,
     )
 

time: 279 us -> 244 us (0.87)
  blocking collectives: 50.9 us -> 0 us
  Pallas kernels: 199 us -> 241 us
  starting transfers between devices: 20.7 us -> 0 us
  waiting for transfers between devices: 4.36 us -> 0 us
    all_to_all x2 -> x0, blocking collectives: 50.9 us -> none  [exchange(): lax.all_to_all(block, 'space', split_axis=0, concat_axis=0, tiled=True)]
    pallas_call x1, Pallas kernels: 35 us -> 56 us  [encode(): pl.pallas_call(encode_kernel, out_shape=(jax.ShapeDtypeStruct((ROWS, C),...]
    pallas_call x1, Pallas kernels: 7.18 us -> 28.2 us  [finish(): pl.pallas_call(finish_kernel, out_shape=jax.ShapeDtypeStruct((ROWS, C), B...]
    all_to_all x2 -> x0, starting transfers between devices: 14.3 us -> none  [exchange(): lax.all_to_all(block, 'space', split_axis=0, concat_axis=0, tiled=True)]
    ppermute x2 -> x0, starting transfers between devices: 6.43 us -> none  [the longest x1 4.51 us: padded(): low = lax.ppermute(block[block.shape[0] - width:], 'space', forward)]
    ppermute x2 -> x0, waiting for transfers between devices: 4.35 us -> none  [the longest x1 4.35 us: padded(): high = lax.ppermute(block[:width], 'space', backward)]
  transfers between devices with their start and end apart: 4 -> 0, of which waited for: 1 -> 0; matrix products, arithmetic and copies ran while one was open for 0% -> 0% of each run, Pallas kernels for 56% -> 0%
where the time goes in v1:
time: 244 us; the launch traced here: 243 us
  Pallas kernels  241 us (99%)
    pallas_call x2, Pallas kernels, attend(): pl.pallas_call(attend_kernel, out_shape=WIRE, scratch_shapes=[pltpu.VMEM(...  157 us
    pallas_call x1, Pallas kernels, encode(): pl.pallas_call(encode_kernel, out_shape=(jax.ShapeDtypeStruct((ROWS, C),...  56 us
    pallas_call x1, Pallas kernels, finish(): pl.pallas_call(finish_kernel, out_shape=jax.ShapeDtypeStruct((ROWS, C), B...  28.2 us

profile of v1, /device:TPU:1, one launch (start us, length us, event | category | flops | bytes accessed | tf_op | source)
XLA Modules:
  0.0 243.4 jit_solution(16752578681034884529)
XLA Ops:
  0.0 56.0 %encode.1 = (bf16[1536,256]{1,0:T(8,128)(2,1)}, bf16[128,16,128]{2,1,0:T(8,128)(2,1)}, bf16[128,16,128]{2,1,0:T(8,128)(2,1)}, s32[1,1536]{1,0:T(1,128)}) custom-call(bf16[1536,256]{1,0:T(8,128)(2,1)} %feats.1, s32[27,1536]{1,0:T(8,128)} %brick.1, s32[27,1536]{1,0:T(8,128)} %row.1, s32[27,1536]{1,0:T(8,128)} %valid.1, s32[1,1536]{1,0:T(1,128)} %bitcast.7, ...), custom_call_target="tpu_custom_call" | custom-call | tf_op jit(solution)/shard_map/encode/pallas_call | solution.py:305
  56.0 78.4 %attend.2.attended0 = bf16[128,16,128]{2,1,0:T(8,128)(2,1)} custom-call(bf16[128,16,128]{2,1,0:T(8,128)(2,1)} %get-tuple-element.9.arrived, f32[1,256]{1,0:T(1,128)} %bitcast.12, f32[1,256]{1,0:T(1,128)} %bitcast.14, bf16[256,768]{1,0:T(8,128)(2,1)} %qkv_weight.3, bf16[256,256]{1,0:T(8,128)(2,1)} %proj.3), custom_call_target="tpu_custom_call" | custom-call | flops 20000000000 | bytes 2097152 | tf_op jit(solution)/shard_map/attend/pallas_call | solution.py:331
  134.5 78.7 %attend.3.attended1 = bf16[128,16,128]{2,1,0:T(8,128)(2,1)} custom-call(bf16[128,16,128]{2,1,0:T(8,128)(2,1)} %get-tuple-element.10.arrived, f32[1,256]{1,0:T(1,128)} %bitcast.13, f32[1,256]{1,0:T(1,128)} %bitcast.15, bf16[256,768]{1,0:T(8,128)(2,1)} %qkv_weight.3, bf16[256,256]{1,0:T(8,128)(2,1)} %proj.3), custom_call_target="tpu_custom_call" | custom-call | flops 20000000000 | bytes 2097152 | tf_op jit(solution)/shard_map/attend/pallas_call | solution.py:331
  213.1 28.2 %finish.1 = bf16[1536,256]{1,0:T(8,128)(2,1)} custom-call(bf16[128,16,128]{2,1,0:T(8,128)(2,1)} %attend.2.attended0, bf16[128,16,128]{2,1,0:T(8,128)(2,1)} %attend.3.attended1, bf16[1536,256]{1,0:T(8,128)(2,1)} %get-tuple-element.11.enriched, s32[1,1536]{1,0:T(1,128)} %get-tuple-element.12.position, f32[1,256]{1,0:T(1,128)} %bitcast.10, f32[1,256]{1,0:T(1,128)} %bitcast.11, ...), custom_call_target="tpu_custom_call" | custom-call | tf_op jit(solution)/shard_map/finish/pallas_call | solution.py:347
  241.3 2.1 copy.19

commit v2 on v1

v2 whole, which is shorter than its diff:
```python
import jax
import jax.numpy as jnp
from jax import lax
from jax.experimental import pallas as pl
from jax.experimental.pallas import tpu as pltpu
from jax.sharding import PartitionSpec as P

HEADS = 16
HEAD = 16
C = 256
PATCH = 1024
BR = 64
HB = 4
PATCH_DEV = 2
KOFF = 27
DEVICES = 128
ROWS = 1536
GROUP = 256
WINDOW = 768
LOG2E = 1.4426950408889634
SAFE_SCORE = 60.0
EMPTY = 1024.0
MARK = 1e38
F32 = jnp.float32
BF16 = jnp.bfloat16


def layer_norm(values, gain, shift):
    average = jnp.mean(values, axis=-1, keepdims=True)
    centred = values - average
    spread = jnp.mean(centred * centred, axis=-1, keepdims=True)
    return centred * lax.rsqrt(spread + 1e-05) * gain + shift


def to_wire(rows):
    shaped = rows.reshape(128, 8, C)
    return jnp.concatenate([shaped[:, :, :128], shaped[:, :, 128:]], axis=1).astype(BF16)


def from_wire(block):
    wide = block.astype(F32)
    return jnp.concatenate([wide[:, :8], wide[:, 8:]], axis=2).reshape(PATCH, C)


def greet(barrier):
    me = lax.axis_index("space")

    def signal(step, carry):
        pl.semaphore_signal(
            barrier, inc=1, device_id=(lax.rem(me + step, DEVICES),),
            device_id_type=pl.DeviceIdType.MESH,
        )
        return carry

    lax.fori_loop(1, DEVICES, signal, 0)


def send_all(source, target, send_sem, recv_sem):
    me = lax.axis_index("space")

    def start(step, carry):
        other = lax.rem(me + step, DEVICES)
        pltpu.make_async_remote_copy(
            src_ref=source.at[other], dst_ref=target.at[me], send_sem=send_sem, recv_sem=recv_sem,
            device_id=(other,), device_id_type=pl.DeviceIdType.MESH,
        ).start()
        return carry

    lax.fori_loop(1, DEVICES, start, 0)
    pltpu.make_async_copy(source.at[me], target.at[me], recv_sem).start()


def wait_all(source, target, send_sem, recv_sem):
    sent = source.at[pl.ds(0, DEVICES - 1)]
    pltpu.make_async_copy(sent, sent, send_sem).wait()
    pltpu.make_async_copy(target, target, recv_sem).wait()


def encode(
    feats, brick, row, valid, dest, weight, linear, gain, shift,
    enriched, outgoing, arrived, position,
    ext_t, weight_t, relative, picked, low, high, send_sem, recv_sem,
):
    me = lax.axis_index("space")
    barrier = pltpu.get_barrier_semaphore()
    greet(barrier)

    own_t = HB * BR // GROUP
    for i in range(ROWS // GROUP):
        ext_t[:, GROUP * (i + own_t) : GROUP * (i + own_t + 1)] = feats[GROUP * i : GROUP * (i + 1), :].T

    def turn_weight(k, carry):
        weight_t[:, pl.ds(pl.multiple_of(k * C, C), C)] = weight[k].T
        return carry

    lax.fori_loop(0, KOFF, turn_weight, 0)
    base = lax.broadcasted_iota(jnp.int32, (KOFF, ROWS), 1) // GROUP * GROUP
    reach = brick[...] * BR + row[...]
    lowest = jnp.where(me == 0, HB * BR, 0)
    highest = jnp.where(me == DEVICES - 1, ROWS + HB * BR, ROWS + 2 * HB * BR)
    counted = (valid[...] > 0) & (reach >= lowest) & (reach < highest)
    relative[...] = jnp.where(counted, reach - base, -1)
    place = lax.broadcasted_iota(jnp.int32, (WINDOW, 1), 0)

    def conv_group(g):
        columns = pl.ds(pl.multiple_of(g * GROUP, GROUP), GROUP)
        window = ext_t[:, pl.ds(pl.multiple_of(g * GROUP, GROUP), WINDOW)]
        for k in range(KOFF):
            chosen = jnp.where(relative[k : k + 1, columns] == place, 1.0, 0.0).astype(BF16)
            picked[C * k : C * (k + 1), :] = jnp.dot(
                window, chosen, preferred_element_type=F32
            ).astype(BF16)
        summed = jnp.dot(weight_t[...], picked[...], preferred_element_type=F32)
        convolved = summed.astype(BF16).T
        projected = jnp.dot(convolved, linear[...], preferred_element_type=F32)
        own = feats[columns, :].astype(F32)
        enriched[columns, :] = (own + layer_norm(projected, gain[...], shift[...])).astype(BF16)

    def inner_group(g, carry):
        conv_group(g)
        return carry

    lax.fori_loop(1, 3, inner_group, 0)
    pl.semaphore_wait(barrier, DEVICES - 1)
    width = HB * BR
    up = pltpu.make_async_remote_copy(
        src_ref=feats.at[pl.ds(ROWS - width, width)], dst_ref=low, send_sem=send_sem.at[4],
        recv_sem=recv_sem.at[4], device_id=(lax.rem(me + 1, DEVICES),),
        device_id_type=pl.DeviceIdType.MESH,
    )
    down = pltpu.make_async_remote_copy(
        src_ref=feats.at[pl.ds(0, width)], dst_ref=high, send_sem=send_sem.at[5],
        recv_sem=recv_sem.at[5], device_id=(lax.rem(me + DEVICES - 1, DEVICES),),
        device_id_type=pl.DeviceIdType.MESH,
    )
    up.start()
    down.start()
    lax.fori_loop(3, 5, inner_group, 0)
    up.wait()
    down.wait()
    ext_t[:, :GROUP] = low[...].T
    ext_t[:, ROWS + GROUP :] = high[...].T

    def outer_group(i, carry):
        conv_group(i * (ROWS // GROUP - 1))
        return carry

    lax.fori_loop(0, 2, outer_group, 0)

    owner = lax.broadcasted_iota(jnp.int32, (128, 1), 0)
    before = jnp.where(
        lax.broadcasted_iota(jnp.int32, (GROUP, GROUP), 0)
        < lax.broadcasted_iota(jnp.int32, (GROUP, GROUP), 1), 1.0, 0.0,
    ).astype(BF16)
    count = jnp.zeros((128, 1), F32)
    for b in range(ROWS // GROUP):
        part = slice(GROUP * b, GROUP * (b + 1))
        target = dest[0:1, part]
        named = jnp.where(target == owner, 1.0, 0.0)
        running = jnp.dot(named.astype(BF16), before, preferred_element_type=F32) + count
        slot = jnp.sum(running * named, axis=0, keepdims=True).astype(jnp.int32)
        count = count + jnp.sum(named, axis=1, keepdims=True)
        position[0:1, part] = jnp.where(slot < 8, 0, PATCH) + target * 8 + slot % 8

    counts = jnp.broadcast_to(count, (128, 128)).astype(BF16)
    expand = jnp.where(
        lax.broadcasted_iota(jnp.int32, (PATCH, 128), 0) // 8
        == lax.broadcasted_iota(jnp.int32, (PATCH, 128), 1), 1.0, 0.0,
    ).astype(BF16)
    filled = jnp.dot(expand, counts, preferred_element_type=F32)
    filled = jnp.concatenate([filled, filled], axis=1)
    slots = (lax.broadcasted_iota(jnp.int32, (PATCH, C), 0) % 8).astype(F32)
    where_to = position[...]
    for patch in range(2):
        index = lax.broadcasted_iota(jnp.int32, (PATCH, 1), 0) + patch * PATCH
        chosen = jnp.where(index == where_to, 1.0, 0.0).astype(BF16)
        moved = jnp.dot(chosen, enriched[...], preferred_element_type=F32)
        outgoing[patch] = to_wire(jnp.where(slots + 8.0 * patch < filled, moved, EMPTY))
        send_all(outgoing.at[patch], arrived.at[patch], send_sem.at[patch], recv_sem.at[patch])


def attend(
    arrived, gain, shift, qkv_weight, proj, attended, keys, query_t, value_t, mixed_t
):
    rows = from_wire(arrived[...])
    occupied = rows[:, 0:1] < 0.5 * EMPTY
    rows = jnp.where(occupied, rows, 0.0)
    normed = layer_norm(rows, gain[...], shift[...]).astype(BF16)
    qkv = jnp.dot(normed, qkv_weight[...], preferred_element_type=F32).astype(BF16)
    queries = qkv[:, :C]
    keys[...] = qkv[:, C : 2 * C]
    values = jnp.where(occupied, qkv[:, 2 * C :], BF16(0))
    ones = jnp.broadcast_to(jnp.where(occupied, 1.0, 0.0), (PATCH, 128)).astype(BF16).T

    member = jnp.where(
        lax.broadcasted_iota(jnp.int32, (C, 128), 0) // HEAD
        == lax.broadcasted_iota(jnp.int32, (C, 128), 1), 1.0, 0.0,
    ).astype(BF16)

    def largest_square(table):
        wide = table.astype(F32)
        squares = jnp.dot((wide * wide).astype(BF16), member, preferred_element_type=F32)
        return jnp.max(squares, axis=0, keepdims=True)

    bound = jnp.max(
        largest_square(queries) * largest_square(qkv[:, C : 2 * C]), axis=1, keepdims=True
    ) / HEAD
    safe = bound < SAFE_SCORE * SAFE_SCORE

    turned = (queries * BF16(HEAD ** (-0.5))).T
    values_t = values.T
    channel = lax.broadcasted_iota(jnp.int32, (128, 1), 0) // HEAD
    for h in range(HEADS):
        half, inside = h // 8, h % 8
        query_t[h] = jnp.where(channel == inside, turned[128 * half : 128 * (half + 1), :], BF16(0))
        value_t[h, :HEAD] = values_t[HEAD * h : HEAD * (h + 1), :]
        value_t[h, HEAD:] = ones[:HEAD, :]

    def finish_head(h, products, columns):
        below = products[HEAD : HEAD + 1, :]
        below = jnp.where(below > 0, below, 1.0)
        mixed_t[h, :, columns] = (products[:HEAD, :] / below).astype(BF16)

    block = 512

    def step(t, carry):
        half, column = t // (PATCH // block), t % (PATCH // block)
        columns = pl.ds(pl.multiple_of(column * block, block), block)
        some = keys[:, pl.ds(pl.multiple_of(half * 128, 128), 128)]
        for inside in range(8):
            h = half * 8 + inside
            scores = jnp.dot(some, query_t[h, :, columns], preferred_element_type=F32)
            weights = jnp.exp2(scores * LOG2E).astype(BF16)
            finish_head(h, jnp.dot(value_t[h], weights, preferred_element_type=F32), columns)
        return carry

    lax.fori_loop(0, 2 * (PATCH // block), step, 0)
    mixed = mixed_t[...].reshape(C, PATCH).T
    result = jnp.dot(mixed, proj[...], preferred_element_type=F32)
    attended[...] = to_wire(jnp.where(jnp.broadcast_to(safe, (PATCH, 1)), result, MARK))


def transform(rows, attended, gain, shift, fc1, fc2, block_t):
    for b in range(PATCH // GROUP):
        part = slice(GROUP * b, GROUP * (b + 1))
        residual = rows[part] + attended[part]
        normed = layer_norm(residual, gain[...], shift[...]).astype(BF16)
        inner = jnp.dot(normed, fc1[...], preferred_element_type=F32)
        hidden = (0.5 * inner * (1.0 + lax.erf(inner * (0.5 ** 0.5)))).astype(BF16)
        finished = residual + jnp.dot(hidden, fc2[...], preferred_element_type=F32)
        block_t[:, part] = finished.astype(BF16).T


def block_kernel(
    feats, brick, row, valid, dest, weight, linear, cpe_gain, cpe_shift, norm1_gain, norm1_shift,
    qkv_weight, proj, norm2_gain, norm2_shift, fc1, fc2,
    output, marked,
    enriched, outgoing, arrived, attended, returned, position,
    ext_t, weight_t, relative, picked, low, high,
    keys, query_t, value_t, mixed_t, block_t, home_t, chosen, send_sem, recv_sem,
):
    encode(
        feats, brick, row, valid, dest, weight, linear, cpe_gain, cpe_shift,
        enriched, outgoing, arrived, position,
        ext_t, weight_t, relative, picked, low, high, send_sem, recv_sem,
    )

    def own_patch(patch, carry):
        wait_all(outgoing.at[patch], arrived.at[patch], send_sem.at[patch], recv_sem.at[patch])
        attend(
            arrived.at[patch], norm1_gain, norm1_shift, qkv_weight, proj, attended.at[patch],
            keys, query_t, value_t, mixed_t,
        )
        send_all(
            attended.at[patch], returned.at[patch], send_sem.at[2 + patch], recv_sem.at[2 + patch]
        )
        return carry

    lax.fori_loop(0, 2, own_patch, 0)

    index = lax.broadcasted_iota(jnp.int32, (2 * PATCH, 1), 0)
    for b in range(ROWS // GROUP):
        part = slice(GROUP * b, GROUP * (b + 1))
        chosen[:, part] = jnp.where(position[0:1, part] == index, 1.0, 0.0).astype(BF16)
    largest = jnp.zeros((1, C), F32)
    for patch in range(2):
        rows = from_wire(outgoing[patch])
        rows = jnp.where(rows[:, 0:1] < 0.5 * EMPTY, rows, 0.0)
        wait_all(
            attended.at[patch], returned.at[patch], send_sem.at[2 + patch], recv_sem.at[2 + patch]
        )
        back = from_wire(returned[patch])
        largest = jnp.maximum(largest, jnp.max(back, axis=0, keepdims=True))
        transform(rows, back, norm2_gain, norm2_shift, fc1, fc2, block_t)
        for b in range(ROWS // GROUP):
            part = slice(GROUP * b, GROUP * (b + 1))
            home = jnp.dot(
                block_t[...], chosen[PATCH * patch : PATCH * (patch + 1), part],
                preferred_element_type=F32,
            )
            if patch == 0:
                home_t[:, part] = home
            else:
                output[part, :] = (home_t[:, part] + home).astype(BF16).T
    marked[...] = jnp.broadcast_to(largest, (8, C))


VMEM = pl.BlockSpec(memory_space=pltpu.VMEM)
WIRE = (2, DEVICES, 16, 128)


def fused(*operands):
    return pl.pallas_call(
        block_kernel,
        out_shape=(
            jax.ShapeDtypeStruct((ROWS, C), BF16),
            jax.ShapeDtypeStruct((8, C), F32),
        ),
        in_specs=[VMEM] * 17,
        out_specs=(VMEM, VMEM),
        scratch_shapes=[
            pltpu.VMEM((ROWS, C), BF16),
            pltpu.VMEM(WIRE, BF16),
            pltpu.VMEM(WIRE, BF16),
            pltpu.VMEM(WIRE, BF16),
            pltpu.VMEM(WIRE, BF16),
            pltpu.VMEM((1, ROWS), jnp.int32),
            pltpu.VMEM((C, 2048), BF16),
            pltpu.VMEM((C, KOFF * C), BF16),
            pltpu.VMEM((KOFF, ROWS), jnp.int32),
            pltpu.VMEM((KOFF * C, GROUP), BF16),
            pltpu.VMEM((HB * BR, C), BF16),
            pltpu.VMEM((HB * BR, C), BF16),
            pltpu.VMEM((PATCH, C), BF16),
            pltpu.VMEM((HEADS, 128, PATCH), BF16),
            pltpu.VMEM((HEADS, 2 * HEAD, PATCH), BF16),
            pltpu.VMEM((HEADS, HEAD, PATCH), BF16),
            pltpu.VMEM((C, PATCH), BF16),
            pltpu.VMEM((C, ROWS), F32),
            pltpu.VMEM((2 * PATCH, ROWS), BF16),
            pltpu.SemaphoreType.DMA((6,)),
            pltpu.SemaphoreType.DMA((6,)),
        ],
        compiler_params=pltpu.CompilerParams(
            collective_id=0, has_side_effects=True, vmem_limit_bytes=58 * 2**20
        ),
        name="block",
    )(*operands)


def padded(block, sides, width):
    for axis, dim in sides:
        count = lax.axis_size(axis)
        forward = [(i, i + 1) for i in range(count - 1)]
        backward = [(target, source) for source, target in forward]
        low = lax.ppermute(
            lax.slice_in_dim(block, block.shape[dim] - width, None, axis=dim), axis, forward
        )
        high = lax.ppermute(lax.slice_in_dim(block, 0, width, axis=dim), axis, backward)
        block = jnp.concatenate([low, block, high], axis=dim)
    return block


def plain_attend(queries, keys, values, occupied):
    slot_count = queries.shape[0]
    patches = slot_count // PATCH
    groups = HEADS // 4

    def arrange(table):
        shaped = table.reshape(patches, PATCH, groups, 4, HEAD).transpose(0, 2, 1, 3, 4)
        return shaped.reshape(patches * groups, PATCH, 4, HEAD)

    masks = jnp.repeat(occupied.reshape(patches, PATCH), groups, axis=0)

    def one_group(items):
        query_part, key_part, value_part, mask_part = items
        scores = jnp.einsum(
            "qhd,khd->hqk", query_part, key_part, preferred_element_type=jnp.float32
        ) * HEAD ** (-0.5)
        scores = jnp.where(mask_part[None, None, :] > 0, scores, -1e30)
        highest = jnp.max(scores, axis=-1, keepdims=True)
        weights = jnp.exp(scores - highest)
        probable = (weights / jnp.sum(weights, axis=-1, keepdims=True)).astype(BF16)
        mixed = jnp.einsum("hqk,khd->qhd", probable, value_part, preferred_element_type=jnp.float32)
        return mixed.astype(BF16)

    mixed = lax.map(one_group, (arrange(queries), arrange(keys), arrange(values), masks))
    mixed = mixed.reshape(patches, groups, PATCH, 4, HEAD).transpose(0, 2, 1, 3, 4)
    return mixed.reshape(slot_count, HEADS * HEAD)


def plain_finish(base_rows, attended, norm2_gain, norm2_shift, fc1_weight, fc2_weight):
    residual = base_rows.astype(jnp.float32) + attended.astype(jnp.float32)
    normed_two = layer_norm(residual, norm2_gain, norm2_shift).astype(BF16)
    hidden = jax.nn.gelu(
        jnp.dot(normed_two, fc1_weight, preferred_element_type=jnp.float32), approximate=False
    ).astype(BF16)
    return (residual + jnp.dot(hidden, fc2_weight, preferred_element_type=jnp.float32)).astype(
        BF16
    )


def plain_block(
    feats,
    nbr_brick,
    nbr_row,
    nbr_valid,
    dest,
    conv_weight,
    cpe_linear,
    cpe_gain,
    cpe_shift,
    norm1_gain,
    norm1_shift,
    qkv_weight,
    proj_weight,
    norm2_gain,
    norm2_shift,
    fc1_weight,
    fc2_weight,
):
    channels = feats.shape[1]
    extended = padded(feats, (("space", 0),), HB * BR)
    neighbour = nbr_brick * BR + nbr_row
    picked = jnp.take(extended, neighbour, axis=0)
    picked = jnp.where(nbr_valid[:, :, None] > 0, picked, jnp.zeros((), BF16))
    convolved = jnp.einsum(
        "krc,kcd->rd", picked, conv_weight, preferred_element_type=jnp.float32
    ).astype(BF16)
    projected = jnp.dot(convolved, cpe_linear, preferred_element_type=jnp.float32)
    enriched = (feats.astype(jnp.float32) + layer_norm(projected, cpe_gain, cpe_shift)).astype(
        BF16
    )
    devices = lax.axis_size("space")
    slot_count = PATCH_DEV * PATCH
    capacity = slot_count // devices
    target = dest[:, 0]
    onehot = (target[:, None] == jnp.arange(devices, dtype=jnp.int32)[None, :]).astype(jnp.int32)
    running = jnp.cumsum(onehot, axis=0)
    within = jnp.sum((running - 1) * onehot, axis=1)
    position = target * capacity + within
    outgoing = jnp.zeros((devices * capacity, channels), BF16).at[position].set(enriched)
    flags_out = jnp.zeros((devices * capacity,), jnp.int32).at[position].set(1)
    arrived, flags_in = (
        lax.all_to_all(outgoing, "space", split_axis=0, concat_axis=0, tiled=True),
        lax.all_to_all(flags_out, "space", split_axis=0, concat_axis=0, tiled=True),
    )
    placed = (
        arrived.reshape(devices, capacity, channels)
        .transpose(1, 0, 2)
        .reshape(slot_count, channels)
    )
    occupied = flags_in.reshape(devices, capacity).transpose(1, 0).reshape(slot_count)
    normed = layer_norm(placed.astype(jnp.float32), norm1_gain, norm1_shift).astype(BF16)
    qkv = jnp.dot(normed, qkv_weight, preferred_element_type=jnp.float32).astype(BF16)
    mixed = plain_attend(
        qkv[:, :channels], qkv[:, channels : 2 * channels], qkv[:, 2 * channels :], occupied
    )
    attended = jnp.dot(mixed, proj_weight, preferred_element_type=jnp.float32).astype(BF16)
    finished = plain_finish(placed, attended, norm2_gain, norm2_shift, fc1_weight, fc2_weight)
    returned = lax.all_to_all(
        finished.reshape(capacity, devices, channels)
        .transpose(1, 0, 2)
        .reshape(slot_count, channels),
        "space",
        split_axis=0,
        concat_axis=0,
        tiled=True,
    )
    return jnp.take(returned, position, axis=0)


def per_device(
    feats, nbr_brick, nbr_row, nbr_valid, dest, conv_weight, cpe_linear, cpe_gain, cpe_shift,
    norm1_gain, norm1_shift, qkv_weight, proj_weight, norm2_gain, norm2_shift, fc1_weight,
    fc2_weight,
):
    line = lambda v: v.reshape(1, C)
    output, marked = fused(
        feats, nbr_brick, nbr_row, nbr_valid, dest.reshape(1, ROWS), conv_weight, cpe_linear,
        line(cpe_gain), line(cpe_shift), line(norm1_gain), line(norm1_shift), qkv_weight,
        proj_weight, line(norm2_gain), line(norm2_shift), fc1_weight, fc2_weight,
    )
    return lax.cond(
        marked[0, 0] < 0.1 * MARK,
        lambda: output,
        lambda: plain_block(
            feats, nbr_brick, nbr_row, nbr_valid, dest, conv_weight, cpe_linear, cpe_gain,
            cpe_shift, norm1_gain, norm1_shift, qkv_weight, proj_weight, norm2_gain, norm2_shift,
            fc1_weight, fc2_weight,
        ),
    )


def solution(mesh):
    placed = (
        P("space", None), P(None, "space"), P(None, "space"), P(None, "space"), P("space", None),
        P(), P(), P(), P(), P(), P(), P(), P(), P(), P(), P(), P(),
    )
    return jax.shard_map(
        per_device, mesh=mesh, in_specs=placed, out_specs=P("space", None), check_vma=False
    )
```

time: 244 us -> 539 us (2.21); the launches traced: 243 us -> 529 us
  matrix products: 0 us -> 184 us
  local copies, waits for them, and re-layouts: 2.06 us -> 164 us
  Pallas kernels: 241 us -> 105 us
  waiting for transfers between devices: 0 us -> 38.5 us
  starting transfers between devices: 0 us -> 27.1 us
  other arithmetic: 0 us -> 9.12 us
    pallas_call x4 -> x1, Pallas kernels: 241 us -> 105 us  [fused(): pl.pallas_call(block_kernel, out_shape=(jax.ShapeDtypeStruct((ROWS, C), B...]
    gather x0 -> x2, local copies, waits for them, and re-layouts: none -> 119 us  [the longest x1 114 us: plain_block(): picked = jnp.take(extended, neighbour, axis=0)]
    dot_general x0 -> x13, matrix products: none -> 101 us  [the longest x8 61.7 us: one_group(): jnp.einsum('hqk,khd->qhd', probable, value_part, preferred_element_type=j...]
    sub x0 -> x8, matrix products: none -> 82.3 us  [one_group(): weights = jnp.exp(scores - highest)]
    all_to_all x0 -> x3, waiting for transfers between devices: none -> 38.5 us  [the longest x1 19.4 us: plain_block(): lax.all_to_all(finished.reshape(capacity, devices, channels).transpose(1,...]
    all_to_all x0 -> x3, starting transfers between devices: none -> 22.8 us  [the longest x1 10.1 us: plain_block(): lax.all_to_all(outgoing, 'space', split_axis=0, concat_axis=0, tiled=True)]
    scatter x0 -> x2, local copies, waits for them, and re-layouts: none -> 14.4 us  [the longest x1 8.18 us: plain_block(): jnp.zeros((devices * capacity, channels), BF16).at[position].set(enriched)]
    reshape x0 -> x7, local copies, waits for them, and re-layouts: none -> 8.79 us  [the longest x3 4.79 us: arrange(): table.reshape(patches, PATCH, groups, 4, HEAD).transpose(0, 2, 1, 3, 4)]
  transfers between devices with their start and end apart: 0 -> 5, of which waited for: 0 -> 2; matrix products, arithmetic and copies ran while one was open for 0% -> 28% of each run, Pallas kernels for 0% -> 0%
where the time goes in v2:
time: 539 us; the launch traced here: 529 us
  matrix products  184 us (34%)
  local copies, waits for them, and re-layouts  164 us (30%)
  Pallas kernels  105 us (19%)
  waiting for transfers between devices  38.5 us (7%)
  starting transfers between devices  27.1 us (5%)
  other arithmetic  9.12 us (2%)
    gather x1, local copies, waits for them, and re-layouts, plain_block(): picked = jnp.take(extended, neighbour, axis=0)  114 us
    pallas_call x1, Pallas kernels, fused(): pl.pallas_call(block_kernel, out_shape=(jax.ShapeDtypeStruct((ROWS, C), B...  105 us
    sub x8, matrix products, one_group(): weights = jnp.exp(scores - highest)  82.3 us
    dot_general x8, matrix products, one_group(): jnp.einsum('hqk,khd->qhd', probable, value_part, preferred_element_type=j...  61.7 us
    dot_general x1, matrix products, plain_finish(): jnp.dot(hidden, fc2_weight, preferred_element_type=jnp.float32)  22.1 us
    all_to_all x1, waiting for transfers between devices, plain_block(): lax.all_to_all(finished.reshape(capacity, devices, channels).transpose(1,...  19.4 us
    all_to_all x1, waiting for transfers between devices, plain_block(): lax.all_to_all(outgoing, 'space', split_axis=0, concat_axis=0, tiled=True)  19.1 us
    dot_general x1, matrix products, plain_block(): jnp.einsum('krc,kcd->rd', picked, conv_weight, preferred_element_type=jnp...  15.4 us
  transfers between devices with their start and end apart: 5, of which 2 were waited for; matrix products, arithmetic and copies ran while one was open for 28% of the time, Pallas kernels for 0%

profile of v2, /device:TPU:1, one launch (start us, length us, event | category | flops | bytes accessed | tf_op | source)
XLA Modules:
  0.0 529.5 jit_solution(7499591461821826916)
XLA Ops:
  0.0 105.3 %block.1 = (bf16[1536,256]{1,0:T(8,128)(2,1)}, f32[8,256]{1,0:T(8,128)}) custom-call(bf16[1536,256]{1,0:T(8,128)(2,1)} %feats.1, s32[27,1536]{1,0:T(8,128)} %brick.1, s32[27,1536]{1,0:T(8,128)} %row.1, s32[27,1536]{1,0:T(8,128)} %valid.1, s32[1,1536]{1,0:T(1,128)} %bitcast.148, bf16[27,256,256]{2,1,0:T(8,128)(2,1)} %weight.1, bf16[256,256]{1,0:T(8,128)(2,1)} %linear.1, ...), custom_call_target="tpu_custom_call" | custom-call | tf_op jit(solution)/shard_map/block/pallas_call | solution.py:313
  107.1 419.8 %conditional.1 = (bf16[1536,256]{1,0:T(8,128)(2,1)}) conditional(s32[]{:T(128)} %bitcast.36, (s32[1536,1]{0,1:T(1,128)}, bf16[1536,256]{1,0:T(8,128)(2,1)}, s32[27,1536]{1,0:T(8,128)}, s32[27,1536]{1,0:T(8,128)}, s32[27,1536]{1,0:T(8,128)}, /*index=5*/bf16[27,256,256]{2,1,0:T(8,128)(2,1)}, bf16[256,256]{1,0:T(8,128)(2,1)}, f32[256]{0:T(256)}, ...), branch_computations={%region_0.16_spmd, %region_16.17_spmd} | conditional | flops 9359847424 | bytes 212463936 | solution.py:484
  116.0 6.2 %scatter_custom_fusion.1 = s32[2048]{0:T(1024)S(1)} fusion(s32[1536]{0:T(1024)S(1)} %reduce.6, s32[1536]{0:T(1024)S(1)} %broadcast.246, s32[]{:T(128)} %copy.121), kind=kCustom, calls=%fused_computation.112 | custom fusion | bytes 8196 | tf_op jit(solution)/shard_map/cond/branch_0_fun/scatter | solution.py:443
  122.9 8.4 %all-to-all-start.1 = ((s32[128,16,1]{1,2,0:T(1,128)}), s32[128,16,1]{1,2,0:T(1,128)S(1)}, u32[]{:S(2)}, u32[]{:S(2)}) async-start(s32[128,16,1]{1,2,0:T(1,128)} %bitcast.17), calls=%async_computation.1 | async-start | bytes 131072 | tf_op jit(solution)/shard_map/cond/branch_0_fun/all_to_all | solution.py:446
  132.9 113.9 %gather_fusion = bf16[41472,256]{1,0:T(8,128)(2,1)} fusion(bf16[2048,256]{1,0:T(8,128)(2,1)S(1)} %pad_maximum_fusion, s32[41984]{0:T(1024)S(1)} %pad_clamp_fusion), kind=kCustom, calls=%fused_computation | custom fusion | bytes 42633216 | tf_op jit(solution)/shard_map/cond/branch_0_fun/jit(_take)/gather | solution.py:425
  246.8 15.4 %fusion.66.clone.1.clone.4 = bf16[1536,256]{1,0:T(8,128)(2,1)S(1)} fusion(bf16[27,256,256]{2,1,0:T(8,128)(2,1)} %get-tuple-element.79, bf16[27,1536,256]{2,1,0:T(8,128)(2,1)} %bitcast.134, pred[27,1536]{1,0:T(8,128)(4,1)S(1)} %get-tuple-element.196, pred[27,1536]{1,0:T(8,128)(4,1)S(1)} %get-tuple-element.211), kind=kOutput, calls=%fused_computation.65.clone.clone.clone.clone.clone.1 | convolution fusion | flops 5457444864 | bytes 25641984 | tf_op jit(solution)/shard_map/cond/branch_0_fun/krc,kcd->rd/dot_general | solution.py:427
  263.6 8.2 %scatter_custom_fusion = bf16[2048,256]{1,0:T(8,128)(2,1)} fusion(s32[1536]{0:T(1024)S(1)} %reduce.6, bf16[1536,256]{1,0:T(8,128)(2,1)S(1)} %copy.90, bf16[]{:T(256)} %constant.39.clone), kind=kCustom, calls=%fused_computation.98 | custom fusion | bytes 1048578 | tf_op jit(solution)/shard_map/cond/branch_0_fun/scatter | solution.py:442
  271.8 10.1 %all-to-all-start = ((bf16[128,16,256]{2,1,0:T(8,128)(2,1)}), bf16[128,16,256]{2,1,0:T(8,128)(2,1)S(1)}, u32[]{:S(2)}, u32[]{:S(2)}) async-start(bf16[128,16,256]{2,1,0:T(8,128)(2,1)} %bitcast.10), calls=%async_computation | async-start | bytes 2097152 | tf_op jit(solution)/shard_map/cond/branch_0_fun/all_to_all | solution.py:445
  282.0 19.1 %all-to-all-done = bf16[128,16,256]{2,1,0:T(8,128)(2,1)S(1)} async-done(((bf16[128,16,256]{2,1,0:T(8,128)(2,1)}), bf16[128,16,256]{2,1,0:T(8,128)(2,1)S(1)}, u32[]{:S(2)}, u32[]{:S(2)}) %all-to-all-start) | async-done | bytes 1048608 | tf_op jit(solution)/shard_map/cond/branch_0_fun/all_to_all | solution.py:445
  310.7 2.5 copy.96
  316.3 2.5 copy.100
  323.4 144.3 %while.9 = (s32[]{:T(128)}, bf16[8,1024,4,16]{1,3,2,0:T(8,128)(2,1)}, bf16[8,1024,4,16]{1,3,2,0:T(8,128)(2,1)}, s32[8,1024]{1,0:T(8,128)S(1)}, bf16[8,1024,4,16]...) while((s32[]{:T(128)}, bf16[8,1024,4,16]{1,3,2,0:T(8,128)(2,1)}, ...), condition=%wide.region_13.13_spmd, body=%wide.region_10.12_spmd.sunk | while | flops 293668864 | bytes 34119760 | solution.py:387
  323.5 10.3 %fusion.172 = (f32[4,1024]{1,0:T(4,128)S(1)}, f32[4,1024,1024]{1,2,0:T(8,128)}) fusion(pred[1024]{0:T(1024)(128)(4,1)S(1)} %compare_reduce_fusion.2, bf16[8,1024,4,16]{1,3,2,0:T(8,128)(2,1)S(1)} %get-tuple-element.272, s32[]{:T(128)} %get-tuple-element.260, bf16[8,1024,4,16]{1,3,2,0:T(8,128)(2,1)} %get-tuple-element.271), kind=kOutput, calls=%fused_computation.149.clone.1 | convolution fusion | flops 150995968 | bytes 17057792 | tf_op jit(solution)/shard_map/cond/branch_0_fun/while/body/eval_jaxpr/sub | solution.py:382
  333.7 7.7 %fusion.173 = bf16[8,1024,4,16]{1,3,2,0:T(8,128)(2,1)} fusion(bf16[8,1024,4,16]{1,3,2,0:T(8,128)(2,1)} %get-tuple-element.261, s32[]{:T(128)} %get-tuple-element.260, f32[4,1024,1024]{1,2,0:T(8,128)} %get-tuple-element.251, f32[4,1024]{1,0:T(4,128)S(1)} %get-tuple-element.252, bf16[8,1024,4,16]{1,3,2,0:T(8,128)(2,1)} %get-tuple-element.269), kind=kOutput, calls=%fused_computation.16.clone.1 | convolution fusion | flops 142671872 | bytes 17056768 | tf_op jit(solution)/shard_map/cond/branch_0_fun/while/body/eval_jaxpr/hqk,khd->qhd/dot_general | solution.py:384
  341.5 10.3 %fusion.172 = (f32[4,1024]{1,0:T(4,128)S(1)}, f32[4,1024,1024]{1,2,0:T(8,128)}) fusion(pred[1024]{0:T(1024)(128)(4,1)S(1)} %compare_reduce_fusion.2, bf16[8,1024,4,16]{1,3,2,0:T(8,128)(2,1)S(1)} %get-tuple-element.272, s32[]{:T(128)} %get-tuple-element.260, bf16[8,1024,4,16]{1,3,2,0:T(8,128)(2,1)} %get-tuple-element.271), kind=kOutput, calls=%fused_computation.149.clone.1 | convolution fusion | flops 150995968 | bytes 17057792 | tf_op jit(solution)/shard_map/cond/branch_0_fun/while/body/eval_jaxpr/sub | solution.py:382
  351.8 7.7 %fusion.173 = bf16[8,1024,4,16]{1,3,2,0:T(8,128)(2,1)} fusion(bf16[8,1024,4,16]{1,3,2,0:T(8,128)(2,1)} %get-tuple-element.261, s32[]{:T(128)} %get-tuple-element.260, f32[4,1024,1024]{1,2,0:T(8,128)} %get-tuple-element.251, f32[4,1024]{1,0:T(4,128)S(1)} %get-tuple-element.252, bf16[8,1024,4,16]{1,3,2,0:T(8,128)(2,1)} %get-tuple-element.269), kind=kOutput, calls=%fused_computation.16.clone.1 | convolution fusion | flops 142671872 | bytes 17056768 | tf_op jit(solution)/shard_map/cond/branch_0_fun/while/body/eval_jaxpr/hqk,khd->qhd/dot_general | solution.py:384
  359.5 10.3 %fusion.172 = (f32[4,1024]{1,0:T(4,128)S(1)}, f32[4,1024,1024]{1,2,0:T(8,128)}) fusion(pred[1024]{0:T(1024)(128)(4,1)S(1)} %compare_reduce_fusion.2, bf16[8,1024,4,16]{1,3,2,0:T(8,128)(2,1)S(1)} %get-tuple-element.272, s32[]{:T(128)} %get-tuple-element.260, bf16[8,1024,4,16]{1,3,2,0:T(8,128)(2,1)} %get-tuple-element.271), kind=kOutput, calls=%fused_computation.149.clone.1 | convolution fusion | flops 150995968 | bytes 17057792 | tf_op jit(solution)/shard_map/cond/branch_0_fun/while/body/eval_jaxpr/sub | solution.py:382
  369.8 7.7 %fusion.173 = bf16[8,1024,4,16]{1,3,2,0:T(8,128)(2,1)} fusion(bf16[8,1024,4,16]{1,3,2,0:T(8,128)(2,1)} %get-tuple-element.261, s32[]{:T(128)} %get-tuple-element.260, f32[4,1024,1024]{1,2,0:T(8,128)} %get-tuple-element.251, f32[4,1024]{1,0:T(4,128)S(1)} %get-tuple-element.252, bf16[8,1024,4,16]{1,3,2,0:T(8,128)(2,1)} %get-tuple-element.269), kind=kOutput, calls=%fused_computation.16.clone.1 | convolution fusion | flops 142671872 | bytes 17056768 | tf_op jit(solution)/shard_map/cond/branch_0_fun/while/body/eval_jaxpr/hqk,khd->qhd/dot_general | solution.py:384
  377.6 10.3 %fusion.172 = (f32[4,1024]{1,0:T(4,128)S(1)}, f32[4,1024,1024]{1,2,0:T(8,128)}) fusion(pred[1024]{0:T(1024)(128)(4,1)S(1)} %compare_reduce_fusion.2, bf16[8,1024,4,16]{1,3,2,0:T(8,128)(2,1)S(1)} %get-tuple-element.272, s32[]{:T(128)} %get-tuple-element.260, bf16[8,1024,4,16]{1,3,2,0:T(8,128)(2,1)} %get-tuple-element.271), kind=kOutput, calls=%fused_computation.149.clone.1 | convolution fusion | flops 150995968 | bytes 17057792 | tf_op jit(solution)/shard_map/cond/branch_0_fun/while/body/eval_jaxpr/sub | solution.py:382
  387.8 7.7 %fusion.173 = bf16[8,1024,4,16]{1,3,2,0:T(8,128)(2,1)} fusion(bf16[8,1024,4,16]{1,3,2,0:T(8,128)(2,1)} %get-tuple-element.261, s32[]{:T(128)} %get-tuple-element.260, f32[4,1024,1024]{1,2,0:T(8,128)} %get-tuple-element.251, f32[4,1024]{1,0:T(4,128)S(1)} %get-tuple-element.252, bf16[8,1024,4,16]{1,3,2,0:T(8,128)(2,1)} %get-tuple-element.269), kind=kOutput, calls=%fused_computation.16.clone.1 | convolution fusion | flops 142671872 | bytes 17056768 | tf_op jit(solution)/shard_map/cond/branch_0_fun/while/body/eval_jaxpr/hqk,khd->qhd/dot_general | solution.py:384
  395.6 10.3 %fusion.172 = (f32[4,1024]{1,0:T(4,128)S(1)}, f32[4,1024,1024]{1,2,0:T(8,128)}) fusion(pred[1024]{0:T(1024)(128)(4,1)S(1)} %compare_reduce_fusion.2, bf16[8,1024,4,16]{1,3,2,0:T(8,128)(2,1)S(1)} %get-tuple-element.272, s32[]{:T(128)} %get-tuple-element.260, bf16[8,1024,4,16]{1,3,2,0:T(8,128)(2,1)} %get-tuple-element.271), kind=kOutput, calls=%fused_computation.149.clone.1 | convolution fusion | flops 150995968 | bytes 17057792 | tf_op jit(solution)/shard_map/cond/branch_0_fun/while/body/eval_jaxpr/sub | solution.py:382
  405.9 7.7 %fusion.173 = bf16[8,1024,4,16]{1,3,2,0:T(8,128)(2,1)} fusion(bf16[8,1024,4,16]{1,3,2,0:T(8,128)(2,1)} %get-tuple-element.261, s32[]{:T(128)} %get-tuple-element.260, f32[4,1024,1024]{1,2,0:T(8,128)} %get-tuple-element.251, f32[4,1024]{1,0:T(4,128)S(1)} %get-tuple-element.252, bf16[8,1024,4,16]{1,3,2,0:T(8,128)(2,1)} %get-tuple-element.269), kind=kOutput, calls=%fused_computation.16.clone.1 | convolution fusion | flops 142671872 | bytes 17056768 | tf_op jit(solution)/shard_map/cond/branch_0_fun/while/body/eval_jaxpr/hqk,khd->qhd/dot_general | solution.py:384
  413.6 10.3 %fusion.172 = (f32[4,1024]{1,0:T(4,128)S(1)}, f32[4,1024,1024]{1,2,0:T(8,128)}) fusion(pred[1024]{0:T(1024)(128)(4,1)S(1)} %compare_reduce_fusion.2, bf16[8,1024,4,16]{1,3,2,0:T(8,128)(2,1)S(1)} %get-tuple-element.272, s32[]{:T(128)} %get-tuple-element.260, bf16[8,1024,4,16]{1,3,2,0:T(8,128)(2,1)} %get-tuple-element.271), kind=kOutput, calls=%fused_computation.149.clone.1 | convolution fusion | flops 150995968 | bytes 17057792 | tf_op jit(solution)/shard_map/cond/branch_0_fun/while/body/eval_jaxpr/sub | solution.py:382
  423.9 7.7 %fusion.173 = bf16[8,1024,4,16]{1,3,2,0:T(8,128)(2,1)} fusion(bf16[8,1024,4,16]{1,3,2,0:T(8,128)(2,1)} %get-tuple-element.261, s32[]{:T(128)} %get-tuple-element.260, f32[4,1024,1024]{1,2,0:T(8,128)} %get-tuple-element.251, f32[4,1024]{1,0:T(4,128)S(1)} %get-tuple-element.252, bf16[8,1024,4,16]{1,3,2,0:T(8,128)(2,1)} %get-tuple-element.269), kind=kOutput, calls=%fused_computation.16.clone.1 | convolution fusion | flops 142671872 | bytes 17056768 | tf_op jit(solution)/shard_map/cond/branch_0_fun/while/body/eval_jaxpr/hqk,khd->qhd/dot_general | solution.py:384
  431.7 10.3 %fusion.172 = (f32[4,1024]{1,0:T(4,128)S(1)}, f32[4,1024,1024]{1,2,0:T(8,128)}) fusion(pred[1024]{0:T(1024)(128)(4,1)S(1)} %compare_reduce_fusion.2, bf16[8,1024,4,16]{1,3,2,0:T(8,128)(2,1)S(1)} %get-tuple-element.272, s32[]{:T(128)} %get-tuple-element.260, bf16[8,1024,4,16]{1,3,2,0:T(8,128)(2,1)} %get-tuple-element.271), kind=kOutput, calls=%fused_computation.149.clone.1 | convolution fusion | flops 150995968 | bytes 17057792 | tf_op jit(solution)/shard_map/cond/branch_0_fun/while/body/eval_jaxpr/sub | solution.py:382
  442.0 7.7 %fusion.173 = bf16[8,1024,4,16]{1,3,2,0:T(8,128)(2,1)} fusion(bf16[8,1024,4,16]{1,3,2,0:T(8,128)(2,1)} %get-tuple-element.261, s32[]{:T(128)} %get-tuple-element.260, f32[4,1024,1024]{1,2,0:T(8,128)} %get-tuple-element.251, f32[4,1024]{1,0:T(4,128)S(1)} %get-tuple-element.252, bf16[8,1024,4,16]{1,3,2,0:T(8,128)(2,1)} %get-tuple-element.269), kind=kOutput, calls=%fused_computation.16.clone.1 | convolution fusion | flops 142671872 | bytes 17056768 | tf_op jit(solution)/shard_map/cond/branch_0_fun/while/body/eval_jaxpr/hqk,khd->qhd/dot_general | solution.py:384
  449.7 10.3 %fusion.172 = (f32[4,1024]{1,0:T(4,128)S(1)}, f32[4,1024,1024]{1,2,0:T(8,128)}) fusion(pred[1024]{0:T(1024)(128)(4,1)S(1)} %compare_reduce_fusion.2, bf16[8,1024,4,16]{1,3,2,0:T(8,128)(2,1)S(1)} %get-tuple-element.272, s32[]{:T(128)} %get-tuple-element.260, bf16[8,1024,4,16]{1,3,2,0:T(8,128)(2,1)} %get-tuple-element.271), kind=kOutput, calls=%fused_computation.149.clone.1 | convolution fusion | flops 150995968 | bytes 17057792 | tf_op jit(solution)/shard_map/cond/branch_0_fun/while/body/eval_jaxpr/sub | solution.py:382
  460.0 7.7 %fusion.173 = bf16[8,1024,4,16]{1,3,2,0:T(8,128)(2,1)} fusion(bf16[8,1024,4,16]{1,3,2,0:T(8,128)(2,1)} %get-tuple-element.261, s32[]{:T(128)} %get-tuple-element.260, f32[4,1024,1024]{1,2,0:T(8,128)} %get-tuple-element.251, f32[4,1024]{1,0:T(4,128)S(1)} %get-tuple-element.252, bf16[8,1024,4,16]{1,3,2,0:T(8,128)(2,1)} %get-tuple-element.269), kind=kOutput, calls=%fused_computation.16.clone.1 | convolution fusion | flops 142671872 | bytes 17056768 | tf_op jit(solution)/shard_map/cond/branch_0_fun/while/body/eval_jaxpr/hqk,khd->qhd/dot_general | solution.py:384
  473.3 22.1 %fusion.71 = bf16[2048,256]{1,0:T(8,128)(2,1)S(1)} fusion(f32[2048,256]{1,0:T(8,128)} %copy-done.1, bf16[1024,256]{1,0:T(8,128)(2,1)S(1)} %copy-done.4, bf16[256,1024]{1,0:T(8,128)(2,1)S(1)} %copy-done.3, f32[256]{0:T(256)S(1)} %copy-done.15, f32[256]{0:T(256)S(1)} %copy-done.14, f32[2048]{0:T(1024)S(1)} %add_rsqrt_fusion, f32[2048]{0:T(1024)S(1)} %broadcast_multiply_fusion), kind=kOutput, calls=%fused_computation.69 | convolution fusion | flops 2287468544 | bytes 4212736 | tf_op jit(solution)/shard_map/cond/branch_0_fun/dot_general | solution.py:398
  496.9 4.3 all-to-all-start.2
  501.3 19.4 %all-to-all-done.2 = bf16[128,16,256]{2,1,0:T(8,128)(2,1)S(1)} async-done(((bf16[128,16,256]{2,1,0:T(8,128)(2,1)}), bf16[128,16,256]{2,1,0:T(8,128)(2,1)S(1)}, u32[]{:S(2)}, u32[]{:S(2)}) %all-to-all-start.2) | async-done | bytes 1048608 | tf_op jit(solution)/shard_map/cond/branch_0_fun/all_to_all | solution.py:461
  520.7 4.8 gather_fusion.1
  (104 shorter events, 41.3 us)
Async XLA Ops:
  107.1 25.4 %copy-start = (bf16[1536,256]{1,0:T(8,128)(2,1)S(1)}, bf16[1536,256]{1,0:T(8,128)(2,1)}, u32[]{:S(2)}) copy-start(bf16[1536,256]{1,0:T(8,128)(2,1)} %get-tuple-element.166) | copy-start | bytes 2359300 | tf_op jit(solution)/shard_map/cond
  108.2 24.6 %collective-permute-start = (bf16[256,256]{1,0:T(8,128)(2,1)S(1)}, bf16[256,256]{1,0:T(8,128)(2,1)S(1)}, u32[]{:S(2)}, u32[]{:S(2)}) collective-permute-start(bf16[256,256]{1,0:T(8,128)(2,1)S(1)} %get-tuple-element.203), channel_id=1, source_target_pairs={{0,1},{1,2},{2,3},{3,4},{4,5},{5,6},{6,7},{7,8},{8,9},{9,10},{10,1... | collective-permute-start | bytes 393224 | tf_op jit(solution)/shard_map/cond/branch_0_fun/ppermute | solution.py:356
  110.5 22.3 %collective-permute-start.1 = (bf16[256,256]{1,0:T(8,128)(2,1)S(1)}, bf16[256,256]{1,0:T(8,128)(2,1)S(1)}, u32[]{:S(2)}, u32[]{:S(2)}) collective-permute-start(bf16[256,256]{1,0:T(8,128)(2,1)S(1)} %get-tuple-element.204), channel_id=1, source_target_pairs={{1,0},{2,1},{3,2},{4,3},{5,4},{6,5},{7,6},{8,7},{9,8},{10,9},{11,1... | collective-permute-start | bytes 393224 | tf_op jit(solution)/shard_map/cond/branch_0_fun/ppermute | solution.py:359
  115.9 147.7 %copy-start.7 = (s32[1536]{0:T(1024)}, s32[1536]{0:T(1024)S(1)}, u32[]{:S(2)}) copy-start(s32[1536]{0:T(1024)S(1)} %reduce.6) | copy-start | bytes 18436 | tf_op jit(solution)/shard_map/cond
  122.9 148.9 %all-to-all-start.1 = ((s32[128,16,1]{1,2,0:T(1,128)}), s32[128,16,1]{1,2,0:T(1,128)S(1)}, u32[]{:S(2)}, u32[]{:S(2)}) async-start(s32[128,16,1]{1,2,0:T(1,128)} %bitcast.17), calls=%async_computation.1 | async-start | bytes 131072 | tf_op jit(solution)/shard_map/cond/branch_0_fun/all_to_all | solution.py:446
  246.8 15.4 %copy-start.5 = (bf16[256,256]{1,0:T(8,128)(2,1)S(1)}, bf16[256,256]{1,0:T(8,128)(2,1)}, u32[]{:S(2)}) copy-start(bf16[256,256]{1,0:T(8,128)(2,1)} %get-tuple-element.80) | copy-start | bytes 393220 | tf_op jit(solution)/shard_map/cond
  246.8 16.1 %copy-start.10 = (f32[256]{0:T(256)S(1)}, f32[256]{0:T(256)}, u32[]{:S(2)}) copy-start(f32[256]{0:T(256)} %get-tuple-element.81) | copy-start | bytes 3076 | tf_op jit(solution)/shard_map/cond
  246.8 16.1 %copy-start.11 = (f32[256]{0:T(256)S(1)}, f32[256]{0:T(256)}, u32[]{:S(2)}) copy-start(f32[256]{0:T(256)} %get-tuple-element.82) | copy-start | bytes 3076 | tf_op jit(solution)/shard_map/cond
  262.9 41.0 %copy-start.12 = (f32[256]{0:T(256)S(1)}, f32[256]{0:T(256)}, u32[]{:S(2)}) copy-start(f32[256]{0:T(256)} %get-tuple-element.83) | copy-start | bytes 3076 | tf_op jit(solution)/shard_map/cond
  262.9 41.0 %copy-start.13 = (f32[256]{0:T(256)S(1)}, f32[256]{0:T(256)}, u32[]{:S(2)}) copy-start(f32[256]{0:T(256)} %get-tuple-element.84) | copy-start | bytes 3076 | tf_op jit(solution)/shard_map/cond
  263.6 41.2 %copy-start.2 = (bf16[256,768]{1,0:T(8,128)(2,1)S(1)}, bf16[256,768]{1,0:T(8,128)(2,1)}, u32[]{:S(2)}) copy-start(bf16[256,768]{1,0:T(8,128)(2,1)} %get-tuple-element.85) | copy-start | bytes 1179652 | tf_op jit(solution)/shard_map/cond
  271.8 29.3 %all-to-all-start = ((bf16[128,16,256]{2,1,0:T(8,128)(2,1)}), bf16[128,16,256]{2,1,0:T(8,128)(2,1)S(1)}, u32[]{:S(2)}, u32[]{:S(2)}) async-start(bf16[128,16,256]{2,1,0:T(8,128)(2,1)} %bitcast.10), calls=%async_computation | async-start | bytes 2097152 | tf_op jit(solution)/shard_map/cond/branch_0_fun/all_to_all | solution.py:445
  323.4 147.0 %copy-start.6 = (bf16[256,256]{1,0:T(8,128)(2,1)S(1)}, bf16[256,256]{1,0:T(8,128)(2,1)}, u32[]{:S(2)}) copy-start(bf16[256,256]{1,0:T(8,128)(2,1)} %get-tuple-element.87) | copy-start | bytes 393220 | tf_op jit(solution)/shard_map/cond
  467.7 5.5 %copy-start.3 = (bf16[256,1024]{1,0:T(8,128)(2,1)S(1)}, bf16[256,1024]{1,0:T(8,128)(2,1)}, u32[]{:S(2)}) copy-start(bf16[256,1024]{1,0:T(8,128)(2,1)} %get-tuple-element.90) | copy-start | bytes 1572868 | tf_op jit(solution)/shard_map/cond
  467.7 5.5 %copy-start.4 = (bf16[1024,256]{1,0:T(8,128)(2,1)S(1)}, bf16[1024,256]{1,0:T(8,128)(2,1)}, u32[]{:S(2)}) copy-start(bf16[1024,256]{1,0:T(8,128)(2,1)} %get-tuple-element.91) | copy-start | bytes 1572868 | tf_op jit(solution)/shard_map/cond
  467.7 5.5 %copy-start.14 = (f32[256]{0:T(256)S(1)}, f32[256]{0:T(256)}, u32[]{:S(2)}) copy-start(f32[256]{0:T(256)} %get-tuple-element.88) | copy-start | bytes 3076 | tf_op jit(solution)/shard_map/cond
  467.7 5.5 %copy-start.15 = (f32[256]{0:T(256)S(1)}, f32[256]{0:T(256)}, u32[]{:S(2)}) copy-start(f32[256]{0:T(256)} %get-tuple-element.89) | copy-start | bytes 3076 | tf_op jit(solution)/shard_map/cond
  471.2 1.4 copy-start.1
  473.3 28.0 %copy-start.8 = (s32[1536]{0:T(1024)S(1)}, s32[1536]{0:T(1024)}, u32[]{:S(2)}) copy-start(s32[1536]{0:T(1024)} %copy-done.7) | copy-start | bytes 18436 | tf_op jit(solution)/shard_map/cond
  495.3 30.1 %copy-start.9 = (pred[1536]{0:T(1024)(128)(4,1)S(1)}, pred[1536]{0:T(1024)(128)(4,1)}, u32[]{:S(2)}) copy-start(pred[1536]{0:T(1024)(128)(4,1)} %get-tuple-element.194) | copy-start | bytes 4612 | tf_op jit(solution)/shard_map/cond
  496.9 23.8 %all-to-all-start.2 = ((bf16[128,16,256]{2,1,0:T(8,128)(2,1)}), bf16[128,16,256]{2,1,0:T(8,128)(2,1)S(1)}, u32[]{:S(2)}, u32[]{:S(2)}) async-start(bf16[128,16,256]{2,1,0:T(8,128)(2,1)} %bitcast.123), calls=%async_computation.2 | async-start | bytes 2097152 | tf_op jit(solution)/shard_map/cond/branch_0_fun/all_to_all | solution.py:461
